TPU v7x, 128 devices: a whole 4x4x4 slice. The times are simulated.
128 devices in a mesh: area: 8 (over x, core), grp: 16 (over z, y).
Axes of the slice: x: 4, y: 4, z: 4, core: 2. Of those that a mesh axis runs over, the one named last changes fastest.
Arguments:
- spikes: int32 [10, 8, 512, 128], P(None, 'area', 'grp'), may hold values 0 or 1
- history: int32 [19, 8, 512, 128], P(None, 'area', 'grp'), may hold values 0 or 1
- intra_source: int32 [8, 16, 64], P('area', 'grp'), may hold values from 0 to 31
- intra_target: int32 [8, 16, 64], P('area', 'grp'), may hold values from 0 to 511, as said below
- intra_weight: float32 [8, 16, 64, 128, 128], P('area', 'grp'), may hold values from -1.25 to 1.25
- inter_area: int32 [8, 16, 48, 1], P('area', 'grp'), may hold values from 0 to 7; in each aligned block of 48 rows (0 to 47, 48 to 95, ..., all dimensions but the last counted through in order) at most 12 rows name the same one
- inter_source: int32 [8, 16, 48], P('area', 'grp'), may hold values from 0 to 31
- inter_block: int32 [8, 16, 48], P('area', 'grp'), may hold values from 0 to 511
- inter_delay: int32 [8, 16, 48], P('area', 'grp'), may hold values from 0 to 9
- inter_weight: float32 [8, 16, 48, 128, 128], P('area', 'grp'), may hold values from -1.25 to 1.25
- voltage_init: float32 [8, 512, 128], P('area', 'grp'), may hold values from -6 to 6
- synapse_init: float32 [8, 512, 128], P('area', 'grp'), may hold values from -6 to 6
- membrane_rate: float32 [8, 512, 128], P('area', 'grp'), may hold values from 0.05 to 0.5
- synapse_decay: float32 [8, 512, 128], P('area', 'grp'), may hold values from 0.4 to 0.9
Outputs:
- voltage: float32 [8, 512, 128], P('area', 'grp')
- synapse: float32 [8, 512, 128], P('area', 'grp')
Inputs may be any that keep to these rules, and one draw needn't show every extreme that they name: `inter_area`: among the 48 tiles of one device no area is named more than 12 times, and some device names one area exactly 12 times. Among the 64 tiles of one device no value of intra_target // 32 occurs more than 8 times, and in every device one value occurs exactly 8 times.
All inputs are finite; a program needn't handle non-finite values. No bound on the sum of `spikes` or of `history` on one device may be relied on, other than what follows from the above.
Results may differ from a plain program's by a relative error of at most 0.0003.
Values sent between devices are 32-bit elements; how exact they have to be, the bound alone decides.
No kernel may reach another device: no remote copies, remote signals or barrier semaphores. Data moves between devices by JAX's collectives and lax.ppermute only.
A program may use at most 64 MiB of HBM per device.

v0:
```python
import functools

import jax
import jax.numpy as jnp
from jax import lax
from jax.experimental import pallas as pl
from jax.experimental.pallas import tpu as pltpu
from jax.sharding import PartitionSpec as P

RESET_LEVEL = -1.0
STEPS = 10
ROOM = 12
SPAN = 128
CHUNK = 16
LIMITS = (60, 4, 8)
MIB = 1 << 20

SMEM = pl.BlockSpec(memory_space=pltpu.SMEM)
VMEM = pl.BlockSpec(memory_space=pltpu.VMEM)
ANY = pl.BlockSpec(memory_space=pl.ANY)


def started(copies):
    copies = list(copies)
    for copy in copies:
        copy.start()
    return copies


def product(rows, weight):
    high = weight.astype(jnp.bfloat16)
    low = (weight - high.astype(jnp.float32)).astype(jnp.bfloat16)
    rows = rows.astype(jnp.float32).astype(jnp.bfloat16)
    both = jnp.concatenate([high, low], axis=0)
    return jnp.dot(jnp.concatenate([rows, rows], axis=1), both, preferred_element_type=jnp.float32)


def first_kernel(blocks, groups, areas, *refs):
    inputs, own, messages, rest = refs[:9], refs[9], refs[10:15], refs[15:]
    area, source, block, delay, spikes, decay, rate, history, weight = rest[:9]
    out, tile, sems, weight_sems, own_sems, out_sems, place, count = rest[9:]
    rows = 3 * blocks
    targets = (
        area,
        source,
        block,
        delay,
        spikes,
        tile.at[pl.ds(0, blocks)],
        tile.at[pl.ds(blocks, blocks)],
        history,
    )
    copies = started(
        pltpu.make_async_copy(inputs[i].at[0] if i in (5, 6) else inputs[i], target, sems.at[i])
        for i, target in enumerate(targets)
    )
    tiles = weight.shape[0]
    weight_copies = started(
        pltpu.make_async_copy(
            inputs[8].at[0, 0, pl.ds(c * CHUNK, CHUNK)], weight.at[pl.ds(c * CHUNK, CHUNK)], weight_sems.at[c]
        )
        for c in range(tiles // CHUNK)
    )
    out[...] = jnp.zeros_like(out)
    for a in range(areas):
        count[a] = 0
    for copy in copies[4:7]:
        copy.wait()
    last = jnp.full((blocks, 128), -1.0, jnp.float32)
    for t in range(STEPS):
        last = jnp.where(spikes[pl.ds(t * blocks, blocks), :] == 1, float(t), last)
    tile[pl.ds(2 * blocks, blocks), :] = last
    own_copies = started(
        pltpu.make_async_copy(tile, own.at[pl.ds(h * rows, rows)], own_sems.at[h]) for h in range(groups)
    )
    for copy in copies[:4]:
        copy.wait()
    me = lax.axis_index("area")
    row = lax.broadcasted_iota(jnp.int32, (areas, 128), 0)
    lane = lax.broadcasted_iota(jnp.int32, (areas, 128), 1)
    names = jnp.full((areas, 128), -1, jnp.int32)
    for k in range(tiles):
        a = area[0, 0, 0, k] ^ me
        rank = count[a]
        count[a] = rank + 1
        place[k] = a * SPAN + rank
        names = jnp.where((row == a) & (lane == rank), block[0, 0, k], names)
    names = names.astype(jnp.float32)
    for a in range(areas):
        out[pl.ds(a * SPAN + STEPS * ROOM, 1), :] = names[a : a + 1, :]
    copies[7].wait()
    for k in range(tiles):
        if k % CHUNK == 0:
            weight_copies[k // CHUNK].wait()
        first = (STEPS - 1 - delay[0, 0, k]) * blocks + source[0, 0, k]
        picked = history[pl.ds(first, STEPS, stride=blocks), :]
        out[pl.ds(place[k], STEPS, stride=ROOM), :] = product(picked, weight[k])
    out_copies = started(
        pltpu.make_async_copy(out.at[pl.ds(first * SPAN, message.shape[0])], message, out_sems.at[j])
        for j, (first, message) in enumerate(zip((0, 1, 2, 4, 6), messages))
    )
    for copy in own_copies + out_copies:
        copy.wait()


def clear_kernel(out):
    out[...] = jnp.zeros_like(out)


def intra_kernel(blocks, source, zeros, spikes, weight, out):
    tiles = weight.shape[2]
    for k in range(tiles):
        rows = spikes[pl.ds(source[0, 0, k], STEPS, stride=blocks), :]
        out[pl.ds(k, STEPS, stride=tiles), :] = product(rows, weight[0, 0, k])
    out[pl.ds(STEPS * tiles, 8), :] = zeros[...]


def contracted(blocks, span, total, params, h):
    base = h * 3 * blocks
    decay = params[pl.ds(base, blocks), :]
    rate = params[pl.ds(base + blocks, blocks), :]
    last = params[pl.ds(base + 2 * blocks, blocks), :]
    synapse = jnp.zeros((blocks, 128), jnp.float32)
    voltage = synapse
    for t in range(STEPS):
        synapse = decay * synapse + total[pl.ds(t * span + h * blocks, blocks), :]
        voltage = voltage + rate * (synapse - voltage)
        voltage = jnp.where(last == float(t), 0.0, voltage)
    return synapse, voltage


def merge_kernel(blocks, groups, areas, span, target, params, intra, *refs):
    arrived = refs[:areas]
    out, total, names, sems = refs[areas:]
    copies = started(
        pltpu.make_async_copy(arrived[a].at[pl.ds(STEPS * ROOM, 1)], names.at[pl.ds(a, 1)], sems.at[a])
        for a in range(areas)
    )
    total[...] = jnp.zeros_like(total)
    tiles = target.shape[2]
    for k in range(tiles):
        spot = pl.ds(target[0, 0, k], STEPS, stride=span)
        total[spot, :] = total[spot, :] + intra[pl.ds(k, STEPS, stride=tiles), :]
    for copy in copies:
        copy.wait()
    for a in range(areas):
        for r in range(ROOM):
            b = names[a, r].astype(jnp.int32)
            spot = pl.ds(jnp.where(b < 0, groups * blocks, b), STEPS, stride=span)
            total[spot, :] = total[spot, :] + arrived[a][pl.ds(r, STEPS, stride=ROOM), :]

    def body(h, _):
        synapse, voltage = contracted(blocks, span, total, params, h)
        out[pl.ds(h * 2 * blocks, blocks), :] = synapse
        out[pl.ds(h * 2 * blocks + blocks, blocks), :] = voltage
        return 0

    lax.fori_loop(0, groups, body, 0, unroll=4)


def finish_kernel(blocks, groups, arrived, spikes, voltage_in, synapse_in, rate_in, decay_in, voltage_out, synapse_out):
    voltage, synapse, rate, decay = voltage_in[0], synapse_in[0], rate_in[0], decay_in[0]
    for t in range(STEPS):
        synapse = decay * synapse
        voltage = voltage + rate * (synapse - voltage)
        voltage = jnp.where(spikes[pl.ds(t * blocks, blocks), :] == 1, RESET_LEVEL, voltage)
    synapse_sum = arrived[pl.ds(0, blocks), :]
    voltage_sum = arrived[pl.ds(blocks, blocks), :]
    for h in range(1, groups):
        synapse_sum += arrived[pl.ds(h * 2 * blocks, blocks), :]
        voltage_sum += arrived[pl.ds(h * 2 * blocks + blocks, blocks), :]
    voltage_out[0] = voltage + voltage_sum
    synapse_out[0] = synapse + synapse_sum


def exchange(rows, axis, parts):
    width = rows.shape[1]
    rows = rows.reshape(parts, -1, width)
    return lax.all_to_all(rows, axis, split_axis=0, concat_axis=0, tiled=True).reshape(-1, width)


def shards(
    spikes,
    history,
    intra_source,
    intra_target,
    intra_weight,
    inter_area,
    inter_source,
    inter_block,
    inter_delay,
    inter_weight,
    voltage_init,
    synapse_init,
    membrane_rate,
    synapse_decay,
):
    blocks, width = spikes.shape[2:]
    groups, areas = lax.axis_size("grp"), lax.axis_size("area")
    spikes = spikes.reshape(STEPS * blocks, width)
    history = history.reshape(-1, width)
    span = groups * blocks + 8
    dma = pltpu.SemaphoreType.DMA

    def shape(rows):
        return jax.ShapeDtypeStruct((rows, width), jnp.float32)

    def params_of(limit):
        return pltpu.CompilerParams(vmem_limit_bytes=limit * MIB)

    def cost(us):
        return pl.CostEstimate(flops=us * 10**9, bytes_accessed=us * 3 * 10**6, transcendentals=0)

    tiles = inter_weight.shape[2]
    own, *messages = pl.pallas_call(
        functools.partial(first_kernel, blocks, groups, areas),
        out_shape=(shape(groups * 3 * blocks),) + (shape(SPAN),) * 2 + (shape(2 * SPAN),) * 3,
        in_specs=[ANY] * 9,
        out_specs=(ANY,) * 6,
        scratch_shapes=[
            pltpu.SMEM((1, 1, 1, tiles), jnp.int32),
            pltpu.SMEM((1, 1, tiles), jnp.int32),
            pltpu.SMEM((1, 1, tiles), jnp.int32),
            pltpu.SMEM((1, 1, tiles), jnp.int32),
            pltpu.VMEM(spikes.shape, jnp.int32),
            pltpu.VMEM((8, width), jnp.float32),
            pltpu.VMEM((8, width), jnp.float32),
            pltpu.VMEM(history.shape, jnp.int32),
            pltpu.VMEM((tiles, width, width), jnp.float32),
            pltpu.VMEM((areas * SPAN, width), jnp.float32),
            pltpu.VMEM((3 * blocks, width), jnp.float32),
            dma((8,)),
            dma((tiles // CHUNK,)),
            dma((groups,)),
            dma((5,)),
            pltpu.SMEM((tiles,), jnp.int32),
            pltpu.SMEM((areas,), jnp.int32),
        ],
        compiler_params=params_of(LIMITS[0]),
        cost_estimate=cost(3),
        name="first",
    )(
        jnp.swapaxes(inter_area, 2, 3),
        inter_source,
        inter_block,
        inter_delay,
        spikes,
        synapse_decay,
        membrane_rate,
        history,
        inter_weight,
    )
    params = exchange(own, "grp", groups)

    def swapped(rows):
        return lax.ppermute(rows, "area", [(i, i ^ 1) for i in range(areas)])

    got = [
        lax.ppermute(messages[j + 1], "area", [(i, i ^ (2 * j)) for i in range(areas)]) for j in (2, 1, 3)
    ]
    arrived = [messages[0], swapped(messages[1])]

    tiles = intra_weight.shape[2]
    zeros = pl.pallas_call(
        clear_kernel,
        out_shape=shape(8),
        out_specs=VMEM,
        compiler_params=params_of(2),
        cost_estimate=cost(6),
        name="clear",
    )()
    intra = pl.pallas_call(
        functools.partial(intra_kernel, blocks),
        out_shape=shape(STEPS * tiles + 8),
        in_specs=[SMEM] + [VMEM] * 3,
        out_specs=VMEM,
        compiler_params=params_of(LIMITS[1]),
        cost_estimate=cost(4),
        name="intra",
    )(intra_source, zeros, spikes, intra_weight)
    *got, intra = lax.optimization_barrier((*got, intra))
    for rows in got:
        arrived += [rows, swapped(rows[SPAN:])]

    message = pl.pallas_call(
        functools.partial(merge_kernel, blocks, groups, areas, span),
        out_shape=shape(groups * 2 * blocks),
        in_specs=[SMEM, VMEM, VMEM] + [VMEM] * areas,
        out_specs=VMEM,
        scratch_shapes=[
            pltpu.VMEM((STEPS * span, width), jnp.float32),
            pltpu.SMEM((areas, 128), jnp.float32),
            dma((areas,)),
        ],
        compiler_params=params_of(LIMITS[2]),
        cost_estimate=cost(2),
        name="merge",
    )(intra_target, params, intra, *arrived)
    sums = exchange(message, "grp", groups)

    return pl.pallas_call(
        functools.partial(finish_kernel, blocks, groups),
        out_shape=(jax.ShapeDtypeStruct(voltage_init.shape, jnp.float32),) * 2,
        in_specs=[VMEM] * 6,
        out_specs=(VMEM, VMEM),
        compiler_params=params_of(LIMITS[2]),
        cost_estimate=cost(1),
        name="finish",
    )(sums, spikes, voltage_init, synapse_init, membrane_rate, synapse_decay)


def solution(mesh):
    in_specs = (
        P(None, "area", "grp", None),
        P(None, "area", "grp", None),
        P("area", "grp", None),
        P("area", "grp", None),
        P("area", "grp", None, None, None),
        P("area", "grp", None, None),
        P("area", "grp", None),
        P("area", "grp", None),
        P("area", "grp", None),
        P("area", "grp", None, None, None),
        P("area", "grp", None),
        P("area", "grp", None),
        P("area", "grp", None),
        P("area", "grp", None),
    )
    out_specs = (P("area", "grp", None), P("area", "grp", None))
    return jax.shard_map(shards, mesh=mesh, in_specs=in_specs, out_specs=out_specs, check_vma=False)
```

profile of v0, /device:TPU:0, one launch (start us, length us, event | category | flops | bytes accessed | tf_op | source)
XLA Modules:
  0.0 46.5 jit_solution(12233093664657407441)
XLA Ops:
  0.6 3.6 %first.1 = (f32[1536,128]{1,0:T(8,128)}, f32[128,128]{1,0:T(8,128)}, f32[128,128]{1,0:T(8,128)}, f32[256,128]{1,0:T(8,128)}, f32[256,128]{1,0:T(8,128)}, /*index=5*/f32[256,128]{1,0:T(8,128)}) custom-call(s32[1,1,1,48]{3,2,1,0:T(1,128)} %bitcast.15, s32[1,1,48]{2,1,0:T(1,128)} %refs_1_.1, s32[1,1,48]{2,1,0:T(1,128)} %refs_2_.1, s32[1,1,48]{2,1,0:T(1,128)} %refs_3_.1, ...), custom_call_target="tpu_custom_call" | custom-call | flops 3000000000 | bytes 9000000 | tf_op jit(solution)/shard_map/first/pallas_call | solution.py:215
  4.3 8.2 %all-to-all-start = ((f32[16,96,128]{2,1,0:T(8,128)}), f32[16,96,128]{2,1,0:T(8,128)S(1)}, u32[]{:S(2)}, u32[]{:S(2)}) async-start(f32[16,96,128]{2,1,0:T(8,128)} %bitcast.13), calls=%async_computation | async-start | bytes 1572864 | tf_op jit(solution)/shard_map/all_to_all | solution.py:179
  12.4 3.1 %collective-permute-start = (f32[256,128]{1,0:T(8,128)}, f32[256,128]{1,0:T(8,128)S(1)}, u32[]{:S(2)}, u32[]{:S(2)}) collective-permute-start(f32[256,128]{1,0:T(8,128)} %get-tuple-element.13), channel_id=1, source_target_pairs={{0,64},{16,80},{32,96},{48,112},{64,0},{80,16},{96,32},{112,48},{1... | collective-permute-start | bytes 393224 | tf_op jit(solution)/shard_map/ppermute | solution.py:259
  15.5 0.6 %collective-permute-start.1 = (f32[256,128]{1,0:T(8,128)}, f32[256,128]{1,0:T(8,128)S(1)}, u32[]{:S(2)}, u32[]{:S(2)}) collective-permute-start(f32[256,128]{1,0:T(8,128)} %get-tuple-element.14), channel_id=1, source_target_pairs={{0,32},{16,48},{32,0},{48,16},{64,96},{80,112},{96,64},{112,80},{1... | collective-permute-start | bytes 393224 | tf_op jit(solution)/shard_map/ppermute | solution.py:259
  16.2 0.5 %collective-permute-start.2 = (f32[256,128]{1,0:T(8,128)}, f32[256,128]{1,0:T(8,128)S(1)}, u32[]{:S(2)}, u32[]{:S(2)}) collective-permute-start(f32[256,128]{1,0:T(8,128)} %get-tuple-element.15), channel_id=1, source_target_pairs={{0,96},{16,112},{32,64},{48,80},{64,32},{80,48},{96,0},{112,16},{1... | collective-permute-start | bytes 393224 | tf_op jit(solution)/shard_map/ppermute | solution.py:259
  16.7 0.0 collective-permute-start.3
  16.7 2.2 %copy-done = f32[1,1,64,128,128]{4,3,2,1,0:T(8,128)S(1)} copy-done((f32[1,1,64,128,128]{4,3,2,1,0:T(8,128)S(1)}, f32[1,1,64,128,128]{4,3,2,1,0:T(8,128)}, u32[]{:S(2)}) %copy-start) | copy-done | bytes 4194328
  18.9 0.0 copy-done.1
  18.9 0.0 copy-done.6
  18.9 1.3 %intra.1 = f32[648,128]{1,0:T(8,128)S(1)} custom-call(s32[1,1,64]{2,1,0:T(1,128)S(1)} %copy-done.6, f32[8,128]{1,0:T(8,128)S(1)} %clear.1.zeros, s32[320,128]{1,0:T(8,128)S(1)} %bitcast.11, f32[1,1,64,128,128]{4,3,2,1,0:T(8,128)S(1)} %copy-done), custom_call_target="tpu_custom_call" | custom-call | flops 4000000000 | bytes 12000000 | tf_op jit(solution)/shard_map/intra/pallas_call | solution.py:272
  20.2 0.1 collective-permute-done.refs_2_
  20.3 1.8 %collective-permute-done.1.refs_4_ = f32[256,128]{1,0:T(8,128)S(1)} collective-permute-done((f32[256,128]{1,0:T(8,128)}, f32[256,128]{1,0:T(8,128)S(1)}, u32[]{:S(2)}, u32[]{:S(2)}) %collective-permute-start.1) | collective-permute-done | bytes 131104 | tf_op jit(solution)/shard_map/ppermute | solution.py:259
  22.1 0.4 collective-permute-done.2.refs_6_
  22.5 0.0 collective-permute-start.4
  22.6 0.5 %collective-permute-start.5 = (f32[128,128]{1,0:T(8,128)S(1)}, f32[128,128]{1,0:T(8,128)S(1)}, u32[]{:S(2)}, u32[]{:S(2)}) collective-permute-start(f32[128,128]{1,0:T(8,128)S(1)} %slice.10), channel_id=1, source_target_pairs={{0,16},{16,0},{32,48},{48,32},{64,80},{80,64},{96,112},{112,96},{1... | collective-permute-start | bytes 196616 | tf_op jit(solution)/shard_map/ppermute | solution.py:256
  23.1 0.1 collective-permute-start.6
  23.2 0.0 collective-permute-done.3.refs_1_
  23.2 0.6 %collective-permute-done.4.refs_3_ = f32[128,128]{1,0:T(8,128)S(1)} collective-permute-done((f32[128,128]{1,0:T(8,128)S(1)}, f32[128,128]{1,0:T(8,128)S(1)}, u32[]{:S(2)}, u32[]{:S(2)}) %collective-permute-start.4) | collective-permute-done | bytes 65568 | tf_op jit(solution)/shard_map/ppermute | solution.py:256
  23.8 0.2 collective-permute-done.5.refs_5_
  24.0 0.4 collective-permute-done.6.refs_7_
  24.3 2.6 %all-to-all-done = f32[16,96,128]{2,1,0:T(8,128)S(1)} async-done(((f32[16,96,128]{2,1,0:T(8,128)}), f32[16,96,128]{2,1,0:T(8,128)S(1)}, u32[]{:S(2)}, u32[]{:S(2)}) %all-to-all-start) | async-done | bytes 786464 | tf_op jit(solution)/shard_map/all_to_all | solution.py:179
  26.9 0.0 copy-done.7
  26.9 0.0 copy-done.8
  27.0 0.0 copy-start.4
  27.0 0.0 copy-start.5
  27.0 2.6 %merge.1 = f32[1024,128]{1,0:T(8,128)S(1)} custom-call(s32[1,1,64]{2,1,0:T(1,128)S(1)} %copy-done.7, f32[1536,128]{1,0:T(8,128)S(1)} %bitcast.7, f32[648,128]{1,0:T(8,128)S(1)} %intra.1, f32[128,128]{1,0:T(8,128)S(1)} %copy-done.8, f32[128,128]{1,0:T(8,128)S(1)} %collective-permute-done.3.refs_1_, f32[256,128]{1,0:T(8,128)S(1)} %collective-permute-done.refs_2_, ...), custom_call_target="tpu_custom_call" | custom-call | flops 2000000000 | bytes 6000000 | tf_op jit(solution)/shard_map/merge/pallas_call | solution.py:285
  29.6 16.2 %all_to_all.10 = f32[16,64,128]{2,1,0:T(8,128)S(1)} all-to-all(f32[16,64,128]{2,1,0:T(8,128)S(1)} %bitcast.8), channel_id=1, replica_groups=mesh['area'=8,'grp'=16] {'grp'}, dimensions={0} | all-to-all | bytes 1048576 | tf_op jit(solution)/shard_map/all_to_all | solution.py:179
  45.8 0.0 copy-done.2
  45.8 0.0 copy-done.3
  45.8 0.0 copy-done.4
  45.8 0.0 copy-done.5
  45.8 0.7 %finish.1 = (f32[1,32,128]{2,1,0:T(8,128)}, f32[1,32,128]{2,1,0:T(8,128)}) custom-call(f32[1024,128]{1,0:T(8,128)S(1)} %bitcast.9, s32[320,128]{1,0:T(8,128)S(1)} %bitcast.12, f32[1,32,128]{2,1,0:T(8,128)S(1)} %copy-done.4, f32[1,32,128]{2,1,0:T(8,128)S(1)} %copy-done.5, f32[1,32,128]{2,1,0:T(8,128)S(1)} %copy-done.3, f32[1,32,128]{2,1,0:T(8,128)S(1)} %copy-done.2), custom_call_target="tpu_custom_call" | custom-call | flops 1000000000 | bytes 3000000 | tf_op jit(solution)/shard_map/finish/pallas_call | solution.py:301
  (11 shorter events, 0.0 us)
Async XLA Ops:
  4.3 22.7 %all-to-all-start = ((f32[16,96,128]{2,1,0:T(8,128)}), f32[16,96,128]{2,1,0:T(8,128)S(1)}, u32[]{:S(2)}, u32[]{:S(2)}) async-start(f32[16,96,128]{2,1,0:T(8,128)} %bitcast.13), calls=%async_computation | async-start | bytes 1572864 | tf_op jit(solution)/shard_map/all_to_all | solution.py:179
  12.4 7.9 %collective-permute-start = (f32[256,128]{1,0:T(8,128)}, f32[256,128]{1,0:T(8,128)S(1)}, u32[]{:S(2)}, u32[]{:S(2)}) collective-permute-start(f32[256,128]{1,0:T(8,128)} %get-tuple-element.13), channel_id=1, source_target_pairs={{0,64},{16,80},{32,96},{48,112},{64,0},{80,16},{96,32},{112,48},{1... | collective-permute-start | bytes 393224 | tf_op jit(solution)/shard_map/ppermute | solution.py:259
  15.5 6.5 %collective-permute-start.1 = (f32[256,128]{1,0:T(8,128)}, f32[256,128]{1,0:T(8,128)S(1)}, u32[]{:S(2)}, u32[]{:S(2)}) collective-permute-start(f32[256,128]{1,0:T(8,128)} %get-tuple-element.14), channel_id=1, source_target_pairs={{0,32},{16,48},{32,0},{48,16},{64,96},{80,112},{96,64},{112,80},{1... | collective-permute-start | bytes 393224 | tf_op jit(solution)/shard_map/ppermute | solution.py:259
  16.2 6.4 %collective-permute-start.2 = (f32[256,128]{1,0:T(8,128)}, f32[256,128]{1,0:T(8,128)S(1)}, u32[]{:S(2)}, u32[]{:S(2)}) collective-permute-start(f32[256,128]{1,0:T(8,128)} %get-tuple-element.15), channel_id=1, source_target_pairs={{0,96},{16,112},{32,64},{48,80},{64,32},{80,48},{96,0},{112,16},{1... | collective-permute-start | bytes 393224 | tf_op jit(solution)/shard_map/ppermute | solution.py:259
  16.7 2.2 %copy-start = (f32[1,1,64,128,128]{4,3,2,1,0:T(8,128)S(1)}, f32[1,1,64,128,128]{4,3,2,1,0:T(8,128)}, u32[]{:S(2)}) copy-start(f32[1,1,64,128,128]{4,3,2,1,0:T(8,128)} %weight.1) | copy-start | bytes 12582916
  16.7 2.2 %copy-start.1 = (s32[10,1,32,128]{3,2,1,0:T(8,128)S(1)}, s32[10,1,32,128]{3,2,1,0:T(8,128)}, u32[]{:S(2)}) copy-start(s32[10,1,32,128]{3,2,1,0:T(8,128)} %param.14) | copy-start | bytes 491524
  16.7 2.2 %copy-start.6 = (s32[1,1,64]{2,1,0:T(1,128)S(1)}, s32[1,1,64]{2,1,0:T(1,128)}, u32[]{:S(2)}) copy-start(s32[1,1,64]{2,1,0:T(1,128)} %source.1) | copy-start | bytes 772
  16.7 6.5 %collective-permute-start.3 = (f32[128,128]{1,0:T(8,128)}, f32[128,128]{1,0:T(8,128)S(1)}, u32[]{:S(2)}, u32[]{:S(2)}) collective-permute-start(f32[128,128]{1,0:T(8,128)} %get-tuple-element.18), channel_id=1, source_target_pairs={{0,16},{16,0},{32,48},{48,32},{64,80},{80,64},{96,112},{112,96},{1... | collective-permute-start | bytes 196616 | tf_op jit(solution)/shard_map/ppermute | solution.py:256
  18.9 8.1 %copy-start.7 = (s32[1,1,64]{2,1,0:T(1,128)S(1)}, s32[1,1,64]{2,1,0:T(1,128)}, u32[]{:S(2)}) copy-start(s32[1,1,64]{2,1,0:T(1,128)} %target.1) | copy-start | bytes 772
  18.9 8.1 %copy-start.8 = (f32[128,128]{1,0:T(8,128)S(1)}, f32[128,128]{1,0:T(8,128)}, u32[]{:S(2)}) copy-start(f32[128,128]{1,0:T(8,128)} %get-tuple-element.17.refs_0_) | copy-start | bytes 196612
  22.5 1.3 %collective-permute-start.4 = (f32[128,128]{1,0:T(8,128)S(1)}, f32[128,128]{1,0:T(8,128)S(1)}, u32[]{:S(2)}, u32[]{:S(2)}) collective-permute-start(f32[128,128]{1,0:T(8,128)S(1)} %slice.9), channel_id=1, source_target_pairs={{0,16},{16,0},{32,48},{48,32},{64,80},{80,64},{96,112},{112,96},{1... | collective-permute-start | bytes 196616 | tf_op jit(solution)/shard_map/ppermute | solution.py:256
  22.6 1.4 %collective-permute-start.5 = (f32[128,128]{1,0:T(8,128)S(1)}, f32[128,128]{1,0:T(8,128)S(1)}, u32[]{:S(2)}, u32[]{:S(2)}) collective-permute-start(f32[128,128]{1,0:T(8,128)S(1)} %slice.10), channel_id=1, source_target_pairs={{0,16},{16,0},{32,48},{48,32},{64,80},{80,64},{96,112},{112,96},{1... | collective-permute-start | bytes 196616 | tf_op jit(solution)/shard_map/ppermute | solution.py:256
  23.1 1.3 %collective-permute-start.6 = (f32[128,128]{1,0:T(8,128)S(1)}, f32[128,128]{1,0:T(8,128)S(1)}, u32[]{:S(2)}, u32[]{:S(2)}) collective-permute-start(f32[128,128]{1,0:T(8,128)S(1)} %slice.11), channel_id=1, source_target_pairs={{0,16},{16,0},{32,48},{48,32},{64,80},{80,64},{96,112},{112,96},{1... | collective-permute-start | bytes 196616 | tf_op jit(solution)/shard_map/ppermute | solution.py:256
  26.9 18.8 %copy-start.2 = (f32[1,32,128]{2,1,0:T(8,128)S(1)}, f32[1,32,128]{2,1,0:T(8,128)}, u32[]{:S(2)}) copy-start(f32[1,32,128]{2,1,0:T(8,128)} %decay_in.1) | copy-start | bytes 49156
  26.9 18.8 %copy-start.3 = (f32[1,32,128]{2,1,0:T(8,128)S(1)}, f32[1,32,128]{2,1,0:T(8,128)}, u32[]{:S(2)}) copy-start(f32[1,32,128]{2,1,0:T(8,128)} %rate_in.1) | copy-start | bytes 49156
  27.0 18.8 %copy-start.4 = (f32[1,32,128]{2,1,0:T(8,128)S(1)}, f32[1,32,128]{2,1,0:T(8,128)}, u32[]{:S(2)}) copy-start(f32[1,32,128]{2,1,0:T(8,128)} %voltage_in.1) | copy-start | bytes 49156
  27.0 18.8 %copy-start.5 = (f32[1,32,128]{2,1,0:T(8,128)S(1)}, f32[1,32,128]{2,1,0:T(8,128)}, u32[]{:S(2)}) copy-start(f32[1,32,128]{2,1,0:T(8,128)} %synapse_in.1) | copy-start | bytes 49156
where the time goes:
time: 46.7 us; the launch traced here: 46.5 us
  blocking collectives  16.2 us (35%)
  starting transfers between devices  13 us (28%)
  Pallas kernels  8.22 us (18%)
  waiting for transfers between devices  6.12 us (13%)
  local copies, waits for them, and re-layouts  2.22 us (5%)
  between operations  0.74 us (2%)
    all_to_all x1, blocking collectives, exchange(): lax.all_to_all(rows, axis, split_axis=0, concat_axis=0, tiled=True)  16.2 us
    all_to_all x1, starting transfers between devices, exchange(): lax.all_to_all(rows, axis, split_axis=0, concat_axis=0, tiled=True)  8.16 us
    ppermute x3, starting transfers between devices, shards(): lax.ppermute(messages[j + 1], 'area', [(i, i ^ 2 * j) for i in range(area...  4.23 us
    pallas_call x1, Pallas kernels, shards(): pl.pallas_call(functools.partial(first_kernel, blocks, groups, areas), ou...  3.65 us
    all_to_all x1, waiting for transfers between devices, exchange(): lax.all_to_all(rows, axis, split_axis=0, concat_axis=0, tiled=True)  2.61 us
    pallas_call x1, Pallas kernels, shards(): pl.pallas_call(functools.partial(merge_kernel, blocks, groups, areas, spa...  2.6 us
    ppermute x3, waiting for transfers between devices, shards(): lax.ppermute(messages[j + 1], 'area', [(i, i ^ 2 * j) for i in range(area...  2.35 us
    unnamed x18, local copies, waits for them, and re-layouts  2.2 us
  transfers between devices with their start and end apart: 8, of which 7 were waited for; matrix products, arithmetic and copies ran while one was open for 0% of the time, Pallas kernels for 3%

commit v1 on v0

--- a/solution.py
+++ b/solution.py
@@ -12,6 +12,7 @@
 ROOM = 12
 SPAN = 128
 CHUNK = 16
+GROUP = 4
 LIMITS = (60, 4, 8)
 MIB = 1 << 20
 
@@ -38,7 +39,7 @@
 def first_kernel(blocks, groups, areas, *refs):
     inputs, own, messages, rest = refs[:9], refs[9], refs[10:15], refs[15:]
     area, source, block, delay, spikes, decay, rate, history, weight = rest[:9]
-    out, tile, sems, weight_sems, own_sems, out_sems, place, count = rest[9:]
+    out, tile, sems, weight_sems, own_sems, out_sems, count = rest[9:]
     rows = 3 * blocks
     targets = (
         area,
@@ -79,40 +80,43 @@
     row = lax.broadcasted_iota(jnp.int32, (areas, 128), 0)
     lane = lax.broadcasted_iota(jnp.int32, (areas, 128), 1)
     names = jnp.full((areas, 128), -1, jnp.int32)
-    for k in range(tiles):
-        a = area[0, 0, 0, k] ^ me
-        rank = count[a]
-        count[a] = rank + 1
-        place[k] = a * SPAN + rank
-        names = jnp.where((row == a) & (lane == rank), block[0, 0, k], names)
-    names = names.astype(jnp.float32)
-    for a in range(areas):
-        out[pl.ds(a * SPAN + STEPS * ROOM, 1), :] = names[a : a + 1, :]
     copies[7].wait()
     for k in range(tiles):
         if k % CHUNK == 0:
             weight_copies[k // CHUNK].wait()
+        a = area[0, 0, 0, k] ^ me
+        a = (a & 1) * 4 + (a >> 1)
+        rank = count[a]
+        count[a] = rank + 1
+        names = jnp.where((row == a) & (lane == rank), block[0, 0, k], names)
         first = (STEPS - 1 - delay[0, 0, k]) * blocks + source[0, 0, k]
         picked = history[pl.ds(first, STEPS, stride=blocks), :]
-        out[pl.ds(place[k], STEPS, stride=ROOM), :] = product(picked, weight[k])
+        out[pl.ds(a * SPAN + rank, STEPS, stride=ROOM), :] = product(picked, weight[k])
+    names = names.astype(jnp.float32)
+    for a in range(areas):
+        out[pl.ds(a * SPAN + STEPS * ROOM, 1), :] = names[a : a + 1, :]
     out_copies = started(
-        pltpu.make_async_copy(out.at[pl.ds(first * SPAN, message.shape[0])], message, out_sems.at[j])
-        for j, (first, message) in enumerate(zip((0, 1, 2, 4, 6), messages))
+        pltpu.make_async_copy(out.at[pl.ds(j * SPAN, n * SPAN)], message.at[pl.ds(0, n * SPAN)], out_sems.at[j])
+        for j, (n, message) in enumerate(zip((1, 1, 1, 1, 4), messages))
     )
     for copy in own_copies + out_copies:
         copy.wait()
 
 
-def clear_kernel(out):
-    out[...] = jnp.zeros_like(out)
-
-
-def intra_kernel(blocks, source, zeros, spikes, weight, out):
+def pack_kernel(across, *refs):
+    outs, sems = refs[3:6], refs[6]
+    for copy in started(
+        pltpu.make_async_copy(across.at[pl.ds((j + 1) * SPAN, SPAN)], out.at[pl.ds(SPAN, SPAN)], sems.at[j])
+        for j, out in enumerate(outs)
+    ):
+        copy.wait()
+
+
+def intra_kernel(blocks, source, spikes, weight, out):
     tiles = weight.shape[2]
     for k in range(tiles):
         rows = spikes[pl.ds(source[0, 0, k], STEPS, stride=blocks), :]
         out[pl.ds(k, STEPS, stride=tiles), :] = product(rows, weight[0, 0, k])
-    out[pl.ds(STEPS * tiles, 8), :] = zeros[...]
 
 
 def contracted(blocks, span, total, params, h):
@@ -129,25 +133,47 @@
     return synapse, voltage
 
 
-def merge_kernel(blocks, groups, areas, span, target, params, intra, *refs):
-    arrived = refs[:areas]
-    out, total, names, sems = refs[areas:]
+def add_rows(total, span, blocks_of, rows_of):
+    spots = [pl.ds(b, STEPS, stride=span) for b in blocks_of]
+    sums = [total[spot, :] for spot in spots]
+    for i, rows in enumerate(rows_of):
+        before = sums[i]
+        for j in range(i):
+            before = jnp.where(blocks_of[i] == blocks_of[j], sums[j], before)
+        sums[i] = before + rows
+    for spot, value in zip(spots, sums):
+        total[spot, :] = value
+
+
+def merge_kernel(blocks, groups, areas, span, target, params, intra, mine, across, *refs):
+    arrived = [(mine, 0), (across, 0)] + [(refs[j], e * SPAN) for j in range(3) for e in range(2)]
+    out, total, names, sems = refs[3:]
     copies = started(
-        pltpu.make_async_copy(arrived[a].at[pl.ds(STEPS * ROOM, 1)], names.at[pl.ds(a, 1)], sems.at[a])
-        for a in range(areas)
+        pltpu.make_async_copy(ref.at[pl.ds(first + STEPS * ROOM, 1)], names.at[pl.ds(a, 1)], sems.at[a])
+        for a, (ref, first) in enumerate(arrived)
     )
     total[...] = jnp.zeros_like(total)
     tiles = target.shape[2]
-    for k in range(tiles):
-        spot = pl.ds(target[0, 0, k], STEPS, stride=span)
-        total[spot, :] = total[spot, :] + intra[pl.ds(k, STEPS, stride=tiles), :]
+    for k in range(0, tiles, GROUP):
+        group = range(k, k + GROUP)
+        add_rows(
+            total,
+            span,
+            [target[0, 0, i] for i in group],
+            [intra[pl.ds(i, STEPS, stride=tiles), :] for i in group],
+        )
     for copy in copies:
         copy.wait()
-    for a in range(areas):
-        for r in range(ROOM):
-            b = names[a, r].astype(jnp.int32)
-            spot = pl.ds(jnp.where(b < 0, groups * blocks, b), STEPS, stride=span)
-            total[spot, :] = total[spot, :] + arrived[a][pl.ds(r, STEPS, stride=ROOM), :]
+    for a, (ref, first) in enumerate(arrived):
+        for r in range(0, ROOM, GROUP):
+            group = range(r, r + GROUP)
+            found = [names[a, i].astype(jnp.int32) for i in group]
+            add_rows(
+                total,
+                span,
+                [jnp.where(b < 0, groups * blocks, b) for b in found],
+                [ref[pl.ds(first + i, STEPS, stride=ROOM), :] for i in group],
+            )
 
     def body(h, _):
         synapse, voltage = contracted(blocks, span, total, params, h)
@@ -212,9 +238,9 @@
         return pl.CostEstimate(flops=us * 10**9, bytes_accessed=us * 3 * 10**6, transcendentals=0)
 
     tiles = inter_weight.shape[2]
-    own, *messages = pl.pallas_call(
+    own, mine, *along, across = pl.pallas_call(
         functools.partial(first_kernel, blocks, groups, areas),
-        out_shape=(shape(groups * 3 * blocks),) + (shape(SPAN),) * 2 + (shape(2 * SPAN),) * 3,
+        out_shape=(shape(groups * 3 * blocks), shape(SPAN)) + (shape(2 * SPAN),) * 3 + (shape(4 * SPAN),),
         in_specs=[ANY] * 9,
         out_specs=(ANY,) * 6,
         scratch_shapes=[
@@ -233,7 +259,6 @@
             dma((tiles // CHUNK,)),
             dma((groups,)),
             dma((5,)),
-            pltpu.SMEM((tiles,), jnp.int32),
             pltpu.SMEM((areas,), jnp.int32),
         ],
         compiler_params=params_of(LIMITS[0]),
@@ -252,40 +277,35 @@
     )
     params = exchange(own, "grp", groups)
 
-    def swapped(rows):
-        return lax.ppermute(rows, "area", [(i, i ^ 1) for i in range(areas)])
-
-    got = [
-        lax.ppermute(messages[j + 1], "area", [(i, i ^ (2 * j)) for i in range(areas)]) for j in (2, 1, 3)
-    ]
-    arrived = [messages[0], swapped(messages[1])]
-
-    tiles = intra_weight.shape[2]
-    zeros = pl.pallas_call(
-        clear_kernel,
-        out_shape=shape(8),
-        out_specs=VMEM,
+    across = lax.ppermute(across, "area", [(i, i ^ 1) for i in range(areas)])
+    packed = pl.pallas_call(
+        pack_kernel,
+        out_shape=(shape(2 * SPAN),) * 3,
+        in_specs=[ANY] * 4,
+        out_specs=(ANY,) * 3,
+        input_output_aliases={1: 0, 2: 1, 3: 2},
+        scratch_shapes=[dma((3,))],
         compiler_params=params_of(2),
         cost_estimate=cost(6),
-        name="clear",
-    )()
+        name="pack",
+    )(across, *along)
+    got = [lax.ppermute(packed[j - 1], "area", [(i, i ^ (2 * j)) for i in range(areas)]) for j in (2, 1, 3)]
+
     intra = pl.pallas_call(
         functools.partial(intra_kernel, blocks),
-        out_shape=shape(STEPS * tiles + 8),
-        in_specs=[SMEM] + [VMEM] * 3,
+        out_shape=shape(STEPS * intra_weight.shape[2]),
+        in_specs=[SMEM] + [VMEM] * 2,
         out_specs=VMEM,
         compiler_params=params_of(LIMITS[1]),
         cost_estimate=cost(4),
         name="intra",
-    )(intra_source, zeros, spikes, intra_weight)
+    )(intra_source, spikes, intra_weight)
     *got, intra = lax.optimization_barrier((*got, intra))
-    for rows in got:
-        arrived += [rows, swapped(rows[SPAN:])]
 
     message = pl.pallas_call(
         functools.partial(merge_kernel, blocks, groups, areas, span),
         out_shape=shape(groups * 2 * blocks),
-        in_specs=[SMEM, VMEM, VMEM] + [VMEM] * areas,
+        in_specs=[SMEM] + [VMEM] * 7,
         out_specs=VMEM,
         scratch_shapes=[
             pltpu.VMEM((STEPS * span, width), jnp.float32),
@@ -295,7 +315,7 @@
         compiler_params=params_of(LIMITS[2]),
         cost_estimate=cost(2),
         name="merge",
-    )(intra_target, params, intra, *arrived)
+    )(intra_target, params, intra, mine, across, *got)
     sums = exchange(message, "grp", groups)
 
     return pl.pallas_call(

time: 46.7 us -> 45.3 us (0.970)
  waiting for transfers between devices: 6.12 us -> 8.66 us
  local copies, waits for them, and re-layouts: 2.22 us -> 0.05 us
  blocking collectives: 16.2 us -> 14.6 us
  starting transfers between devices: 13 us -> 12.5 us
    unnamed x18, local copies, waits for them, and re-layouts: 2.2 us -> 0.05 us
    all_to_all x1, blocking collectives: 16.2 us -> 14.6 us  [exchange(): lax.all_to_all(rows, axis, split_axis=0, concat_axis=0, tiled=True)]
    ppermute x7 -> x4, waiting for transfers between devices: 3.5 us -> 4.99 us  [the longest x3 4.98 us: shards(): lax.ppermute(packed[j - 1], 'area', [(i, i ^ 2 * j) for i in range(areas)])]
    all_to_all x1, waiting for transfers between devices: 2.61 us -> 3.67 us  [exchange(): lax.all_to_all(rows, axis, split_axis=0, concat_axis=0, tiled=True)]
    pallas_call x1, Pallas kernels: 0.01 us -> 0.71 us  [shards(): pl.pallas_call(pack_kernel, out_shape=(shape(2 * SPAN),) * 3, in_specs=[A...]
    ppermute x7 -> x4, starting transfers between devices: 4.82 us -> 4.33 us  [the longest x3 4.25 us: shards(): lax.ppermute(packed[j - 1], 'area', [(i, i ^ 2 * j) for i in range(areas)])]
  transfers between devices with their start and end apart: 8 -> 5, of which waited for: 7 -> 4; matrix products, arithmetic and copies ran while one was open for 0% -> 0% of each run, Pallas kernels for 3% -> 4%
where the time goes in v1:
time: 45.3 us; the launch traced here: 45.1 us
  blocking collectives  14.6 us (32%)
  starting transfers between devices  12.5 us (28%)
  waiting for transfers between devices  8.66 us (19%)
  Pallas kernels  8.59 us (19%)
  between operations  0.75 us (2%)
    all_to_all x1, blocking collectives, exchange(): lax.all_to_all(rows, axis, split_axis=0, concat_axis=0, tiled=True)  14.6 us
    all_to_all x1, starting transfers between devices, exchange(): lax.all_to_all(rows, axis, split_axis=0, concat_axis=0, tiled=True)  8.14 us
    ppermute x3, waiting for transfers between devices, shards(): lax.ppermute(packed[j - 1], 'area', [(i, i ^ 2 * j) for i in range(areas)])  4.98 us
    ppermute x3, starting transfers between devices, shards(): lax.ppermute(packed[j - 1], 'area', [(i, i ^ 2 * j) for i in range(areas)])  4.25 us
    pallas_call x1, Pallas kernels, shards(): pl.pallas_call(functools.partial(first_kernel, blocks, groups, areas), ou...  3.69 us
    all_to_all x1, waiting for transfers between devices, exchange(): lax.all_to_all(rows, axis, split_axis=0, concat_axis=0, tiled=True)  3.67 us
    pallas_call x1, Pallas kernels, shards(): pl.pallas_call(functools.partial(merge_kernel, blocks, groups, areas, spa...  2.22 us
    pallas_call x1, Pallas kernels, shards(): pl.pallas_call(functools.partial(intra_kernel, blocks), out_shape=shape(S...  1.3 us
  transfers between devices with their start and end apart: 5, of which 4 were waited for; matrix products, arithmetic and copies ran while one was open for 0% of the time, Pallas kernels for 4%

profile of v1, /device:TPU:0, one launch (start us, length us, event | category | flops | bytes accessed | tf_op | source)
XLA Modules:
  0.0 45.1 jit_solution(4277418456618720815)
XLA Ops:
  0.6 3.7 %first.1 = (f32[1536,128]{1,0:T(8,128)}, f32[128,128]{1,0:T(8,128)}, f32[256,128]{1,0:T(8,128)}, f32[256,128]{1,0:T(8,128)}, f32[256,128]{1,0:T(8,128)}, /*index=5*/f32[512,128]{1,0:T(8,128)}) custom-call(s32[1,1,1,48]{3,2,1,0:T(1,128)} %bitcast.15, s32[1,1,48]{2,1,0:T(1,128)} %refs_1_.1, s32[1,1,48]{2,1,0:T(1,128)} %refs_2_.1, s32[1,1,48]{2,1,0:T(1,128)} %refs_3_.1, ...), custom_call_target="tpu_custom_call" | custom-call | flops 3000000000 | bytes 9000000 | tf_op jit(solution)/shard_map/first/pallas_call | solution.py:241
  4.3 0.1 collective-permute-start
  4.4 8.1 %all-to-all-start = ((f32[16,96,128]{2,1,0:T(8,128)}), f32[16,96,128]{2,1,0:T(8,128)S(1)}, u32[]{:S(2)}, u32[]{:S(2)}) async-start(f32[16,96,128]{2,1,0:T(8,128)} %bitcast.13), calls=%async_computation | async-start | bytes 1572864 | tf_op jit(solution)/shard_map/all_to_all | solution.py:205
  12.6 0.0 collective-permute-done.across
  12.6 0.0 copy-start
  12.6 0.0 copy-start.1
  12.6 0.0 copy-start.6
  12.6 0.7 %pack.1 = (f32[256,128]{1,0:T(8,128)}, f32[256,128]{1,0:T(8,128)}, f32[256,128]{1,0:T(8,128)}) custom-call(f32[512,128]{1,0:T(8,128)S(1)} %collective-permute-done.across, f32[256,128]{1,0:T(8,128)} %get-tuple-element.17.refs_0_, f32[256,128]{1,0:T(8,128)} %get-tuple-element.18.refs_1_, ...), custom_call_target="tpu_custom_call", output_to_operand_aliasing={{0}: (1, {}), {1}: (2, {}), {2}: (3, {})} | custom-call | flops 6000000000 | bytes 18000000 | tf_op jit(solution)/shard_map/pack/pallas_call | solution.py:281
  13.3 3.1 %collective-permute-start.1 = (f32[256,128]{1,0:T(8,128)}, f32[256,128]{1,0:T(8,128)S(1)}, u32[]{:S(2)}, u32[]{:S(2)}) collective-permute-start(f32[256,128]{1,0:T(8,128)} %get-tuple-element.20), channel_id=1, source_target_pairs={{0,64},{16,80},{32,96},{48,112},{64,0},{80,16},{96,32},{112,48},{1... | collective-permute-start | bytes 393224 | tf_op jit(solution)/shard_map/ppermute | solution.py:292
  16.4 0.6 %collective-permute-start.2 = (f32[256,128]{1,0:T(8,128)}, f32[256,128]{1,0:T(8,128)S(1)}, u32[]{:S(2)}, u32[]{:S(2)}) collective-permute-start(f32[256,128]{1,0:T(8,128)} %get-tuple-element.21), channel_id=1, source_target_pairs={{0,32},{16,48},{32,0},{48,16},{64,96},{80,112},{96,64},{112,80},{1... | collective-permute-start | bytes 393224 | tf_op jit(solution)/shard_map/ppermute | solution.py:292
  17.0 0.0 copy-start.7
  17.0 0.0 copy-start.8
  17.0 0.6 %collective-permute-start.3 = (f32[256,128]{1,0:T(8,128)}, f32[256,128]{1,0:T(8,128)S(1)}, u32[]{:S(2)}, u32[]{:S(2)}) collective-permute-start(f32[256,128]{1,0:T(8,128)} %get-tuple-element.22), channel_id=1, source_target_pairs={{0,96},{16,112},{32,64},{48,80},{64,32},{80,48},{96,0},{112,16},{1... | collective-permute-start | bytes 393224 | tf_op jit(solution)/shard_map/ppermute | solution.py:292
  17.6 0.0 copy-done
  17.6 0.0 copy-done.1
  17.6 0.0 copy-done.6
  17.6 1.3 %intra.1 = f32[640,128]{1,0:T(8,128)S(1)} custom-call(s32[1,1,64]{2,1,0:T(1,128)S(1)} %copy-done.6, s32[320,128]{1,0:T(8,128)S(1)} %bitcast.11, f32[1,1,64,128,128]{4,3,2,1,0:T(8,128)S(1)} %copy-done), custom_call_target="tpu_custom_call" | custom-call | flops 4000000000 | bytes 12000000 | tf_op jit(solution)/shard_map/intra/pallas_call | solution.py:294
  18.9 2.6 %collective-permute-done.1.refs_0_ = f32[256,128]{1,0:T(8,128)S(1)} collective-permute-done((f32[256,128]{1,0:T(8,128)}, f32[256,128]{1,0:T(8,128)S(1)}, u32[]{:S(2)}, u32[]{:S(2)}) %collective-permute-start.1) | collective-permute-done | bytes 131104 | tf_op jit(solution)/shard_map/ppermute | solution.py:292
  21.5 2.2 %collective-permute-done.2.refs_1_ = f32[256,128]{1,0:T(8,128)S(1)} collective-permute-done((f32[256,128]{1,0:T(8,128)}, f32[256,128]{1,0:T(8,128)S(1)}, u32[]{:S(2)}, u32[]{:S(2)}) %collective-permute-start.2) | collective-permute-done | bytes 131104 | tf_op jit(solution)/shard_map/ppermute | solution.py:292
  23.6 0.3 collective-permute-done.3.refs_2_
  23.9 3.7 %all-to-all-done = f32[16,96,128]{2,1,0:T(8,128)S(1)} async-done(((f32[16,96,128]{2,1,0:T(8,128)}), f32[16,96,128]{2,1,0:T(8,128)S(1)}, u32[]{:S(2)}, u32[]{:S(2)}) %all-to-all-start) | async-done | bytes 786464 | tf_op jit(solution)/shard_map/all_to_all | solution.py:205
  27.6 0.0 copy-done.7
  27.6 0.0 copy-done.8
  27.6 0.0 copy-start.4
  27.6 0.0 copy-start.5
  27.6 2.2 %merge.1 = f32[1024,128]{1,0:T(8,128)S(1)} custom-call(s32[1,1,64]{2,1,0:T(1,128)S(1)} %copy-done.7, f32[1536,128]{1,0:T(8,128)S(1)} %bitcast.7, f32[640,128]{1,0:T(8,128)S(1)} %intra.1, f32[128,128]{1,0:T(8,128)S(1)} %copy-done.8, f32[512,128]{1,0:T(8,128)S(1)} %collective-permute-done.across, f32[256,128]{1,0:T(8,128)S(1)} %collective-permute-done.1.refs_0_, ...), custom_call_target="tpu_custom_call" | custom-call | flops 2000000000 | bytes 6000000 | tf_op jit(solution)/shard_map/merge/pallas_call | solution.py:305
  29.8 14.6 %all_to_all.10 = f32[16,64,128]{2,1,0:T(8,128)S(1)} all-to-all(f32[16,64,128]{2,1,0:T(8,128)S(1)} %bitcast.8), channel_id=1, replica_groups=mesh['area'=8,'grp'=16] {'grp'}, dimensions={0} | all-to-all | bytes 1048576 | tf_op jit(solution)/shard_map/all_to_all | solution.py:205
  44.4 0.0 copy-done.2
  44.4 0.0 copy-done.3
  44.4 0.0 copy-done.4
  44.4 0.0 copy-done.5
  44.4 0.7 %finish.1 = (f32[1,32,128]{2,1,0:T(8,128)}, f32[1,32,128]{2,1,0:T(8,128)}) custom-call(f32[1024,128]{1,0:T(8,128)S(1)} %bitcast.9, s32[320,128]{1,0:T(8,128)S(1)} %bitcast.12, f32[1,32,128]{2,1,0:T(8,128)S(1)} %copy-done.4, f32[1,32,128]{2,1,0:T(8,128)S(1)} %copy-done.5, f32[1,32,128]{2,1,0:T(8,128)S(1)} %copy-done.3, f32[1,32,128]{2,1,0:T(8,128)S(1)} %copy-done.2), custom_call_target="tpu_custom_call" | custom-call | flops 1000000000 | bytes 3000000 | tf_op jit(solution)/shard_map/finish/pallas_call | solution.py:321
  (2 shorter events, 0.0 us)
Async XLA Ops:
  4.3 8.2 %collective-permute-start = (f32[512,128]{1,0:T(8,128)}, f32[512,128]{1,0:T(8,128)S(1)}, u32[]{:S(2)}, u32[]{:S(2)}) collective-permute-start(f32[512,128]{1,0:T(8,128)} %get-tuple-element.16), channel_id=1, source_target_pairs={{0,16},{16,0},{32,48},{48,32},{64,80},{80,64},{96,112},{112,96},{1... | collective-permute-start | bytes 786440 | tf_op jit(solution)/shard_map/ppermute | solution.py:280
  4.4 23.1 %all-to-all-start = ((f32[16,96,128]{2,1,0:T(8,128)}), f32[16,96,128]{2,1,0:T(8,128)S(1)}, u32[]{:S(2)}, u32[]{:S(2)}) async-start(f32[16,96,128]{2,1,0:T(8,128)} %bitcast.13), calls=%async_computation | async-start | bytes 1572864 | tf_op jit(solution)/shard_map/all_to_all | solution.py:205
  12.6 5.0 %copy-start = (f32[1,1,64,128,128]{4,3,2,1,0:T(8,128)S(1)}, f32[1,1,64,128,128]{4,3,2,1,0:T(8,128)}, u32[]{:S(2)}) copy-start(f32[1,1,64,128,128]{4,3,2,1,0:T(8,128)} %weight.1) | copy-start | bytes 12582916
  12.6 5.0 %copy-start.1 = (s32[10,1,32,128]{3,2,1,0:T(8,128)S(1)}, s32[10,1,32,128]{3,2,1,0:T(8,128)}, u32[]{:S(2)}) copy-start(s32[10,1,32,128]{3,2,1,0:T(8,128)} %param.14) | copy-start | bytes 491524
  12.6 5.0 %copy-start.6 = (s32[1,1,64]{2,1,0:T(1,128)S(1)}, s32[1,1,64]{2,1,0:T(1,128)}, u32[]{:S(2)}) copy-start(s32[1,1,64]{2,1,0:T(1,128)} %source.1) | copy-start | bytes 772
  13.3 8.1 %collective-permute-start.1 = (f32[256,128]{1,0:T(8,128)}, f32[256,128]{1,0:T(8,128)S(1)}, u32[]{:S(2)}, u32[]{:S(2)}) collective-permute-start(f32[256,128]{1,0:T(8,128)} %get-tuple-element.20), channel_id=1, source_target_pairs={{0,64},{16,80},{32,96},{48,112},{64,0},{80,16},{96,32},{112,48},{1... | collective-permute-start | bytes 393224 | tf_op jit(solution)/shard_map/ppermute | solution.py:292
  16.4 7.2 %collective-permute-start.2 = (f32[256,128]{1,0:T(8,128)}, f32[256,128]{1,0:T(8,128)S(1)}, u32[]{:S(2)}, u32[]{:S(2)}) collective-permute-start(f32[256,128]{1,0:T(8,128)} %get-tuple-element.21), channel_id=1, source_target_pairs={{0,32},{16,48},{32,0},{48,16},{64,96},{80,112},{96,64},{112,80},{1... | collective-permute-start | bytes 393224 | tf_op jit(solution)/shard_map/ppermute | solution.py:292
  17.0 10.5 %copy-start.7 = (s32[1,1,64]{2,1,0:T(1,128)S(1)}, s32[1,1,64]{2,1,0:T(1,128)}, u32[]{:S(2)}) copy-start(s32[1,1,64]{2,1,0:T(1,128)} %target.1) | copy-start | bytes 772
  17.0 10.5 %copy-start.8 = (f32[128,128]{1,0:T(8,128)S(1)}, f32[128,128]{1,0:T(8,128)}, u32[]{:S(2)}) copy-start(f32[128,128]{1,0:T(8,128)} %get-tuple-element.24.mine) | copy-start | bytes 196612
  17.0 6.9 %collective-permute-start.3 = (f32[256,128]{1,0:T(8,128)}, f32[256,128]{1,0:T(8,128)S(1)}, u32[]{:S(2)}, u32[]{:S(2)}) collective-permute-start(f32[256,128]{1,0:T(8,128)} %get-tuple-element.22), channel_id=1, source_target_pairs={{0,96},{16,112},{32,64},{48,80},{64,32},{80,48},{96,0},{112,16},{1... | collective-permute-start | bytes 393224 | tf_op jit(solution)/shard_map/ppermute | solution.py:292
  27.6 16.8 %copy-start.2 = (f32[1,32,128]{2,1,0:T(8,128)S(1)}, f32[1,32,128]{2,1,0:T(8,128)}, u32[]{:S(2)}) copy-start(f32[1,32,128]{2,1,0:T(8,128)} %decay_in.1) | copy-start | bytes 49156
  27.6 16.8 %copy-start.3 = (f32[1,32,128]{2,1,0:T(8,128)S(1)}, f32[1,32,128]{2,1,0:T(8,128)}, u32[]{:S(2)}) copy-start(f32[1,32,128]{2,1,0:T(8,128)} %rate_in.1) | copy-start | bytes 49156
  27.6 16.8 %copy-start.4 = (f32[1,32,128]{2,1,0:T(8,128)S(1)}, f32[1,32,128]{2,1,0:T(8,128)}, u32[]{:S(2)}) copy-start(f32[1,32,128]{2,1,0:T(8,128)} %voltage_in.1) | copy-start | bytes 49156
  27.6 16.8 %copy-start.5 = (f32[1,32,128]{2,1,0:T(8,128)S(1)}, f32[1,32,128]{2,1,0:T(8,128)}, u32[]{:S(2)}) copy-start(f32[1,32,128]{2,1,0:T(8,128)} %synapse_in.1) | copy-start | bytes 49156
